TPU v7x, 128 devices: a whole 4x4x4 slice. The times are simulated.
128 devices in a mesh: blk: 8 (over y_lo, x), vslab: 16 (over z, y_hi, core).
Axes of the slice: x: 4, y: 4 (y_hi: 2, y_lo: 2; y = y_hi * 2 + y_lo), z: 4, core: 2. Of those that a mesh axis runs over, the one named last changes fastest.
Arguments:
- amplitudes: float32 [1024, 128, 800], P('blk', 'vslab'), may hold values from -6 to 6
- integrals: float32 [128, 800, 4096], P('vslab', None, 'blk'), may hold values from -0.01953125 to 0.01953125
- ab_energy: float32 [4096], P('blk'), may hold values from 1 to 4
- ij_energy: float32 [1024], replicated, may hold values from -4 to -1
- block_size: int32 [32], replicated, may hold values from 1 to 95, as said below
- block_owner: int32 [32], replicated, may hold values from 0 to 15, as said below
Outputs:
- amplitude_new: float32 [1024, 12288], P(None, ('blk', 'vslab'))
Inputs may be any that keep to these rules, and one draw needn't show every extreme that they name: `block_size`: the blocks of one group fill its 512 pairs exactly; every owner holds at most 96 pairs, and one owner exactly 96. `block_owner`: every owner has two blocks.
All inputs are finite; a program needn't handle non-finite values.
Results may differ from a plain program's by a relative error of at most 0.00007.
Values sent between devices are 32-bit elements; how exact they have to be, the bound alone decides.
No kernel may reach another device: no remote copies, remote signals or barrier semaphores. Data moves between devices by JAX's collectives and lax.ppermute only.
A program may use at most 128 MiB of HBM per device.

v0:
```python
import jax
import jax.numpy as jnp
from jax import lax
from jax.sharding import PartitionSpec as P


def slot_tables(block_size, block_owner, rows, owners, cap):
    count = block_size.shape[0]
    order = jnp.arange(count, dtype=jnp.int32)
    before_me = order[None, :] < order[:, None]
    starts = jnp.sum(jnp.where(before_me, block_size[None, :], 0), axis=1)
    same = block_owner[:, None] == block_owner[None, :]
    earlier = before_me
    before = jnp.sum(jnp.where(same & earlier, block_size[None, :], 0), axis=1)
    owner_hot = block_owner[:, None] == jnp.arange(owners, dtype=jnp.int32)[None, :]
    load = jnp.sum(jnp.where(owner_hot, block_size[:, None], 0), axis=0)
    owner_ids = jnp.arange(owners, dtype=jnp.int32)
    owner_start = jnp.sum(
        jnp.where(owner_ids[None, :] < owner_ids[:, None], load[None, :], 0), axis=1
    )
    block_base = jnp.sum(jnp.where(owner_hot, owner_start[None, :], 0), axis=1)
    shift_by = block_base + before - starts
    row_ids = jnp.arange(rows, dtype=jnp.int32)
    inside = (row_ids[:, None] >= starts[None, :]) & (
        row_ids[:, None] < (starts + block_size)[None, :]
    )
    position = jnp.sum(jnp.where(inside, shift_by[None, :], 0), axis=1) + row_ids
    perm = jnp.zeros((rows,), jnp.int32).at[position].set(row_ids)
    slot_ids = jnp.arange(cap, dtype=jnp.int32)
    valid = slot_ids[None, :] < load[:, None]
    index = jnp.minimum(owner_start[:, None] + slot_ids[None, :], rows - 1)
    source = perm[index]
    return (perm, owner_start, load, source, valid)


def on_device(amplitudes, integrals, ab_energy, ij_energy, block_size, block_owner):
    owners = lax.axis_size("vslab")
    rows = integrals.shape[2]
    cap = 3 * rows // owners
    v_matrix = integrals.reshape(-1, rows)
    t_tile = amplitudes.reshape(amplitudes.shape[0], -1)
    ladder = jnp.dot(
        lax.all_gather(t_tile, "blk", axis=0, tiled=True),
        v_matrix,
        precision=lax.Precision.HIGHEST,
        preferred_element_type=jnp.float32,
    )
    perm, owner_start, load, source, valid = slot_tables(block_size, block_owner, rows, owners, cap)
    mine = lax.axis_index("vslab")
    my_source = lax.dynamic_index_in_dim(source, mine, 0, keepdims=False)
    my_valid = lax.dynamic_index_in_dim(valid, mine, 0, keepdims=False)
    packed = jnp.take(ladder, source.reshape(-1), axis=1)
    packed = jnp.where(valid.reshape(1, -1), packed, 0.0).reshape(ladder.shape[0], owners, cap)
    received = lax.all_to_all(packed, "vslab", split_axis=1, concat_axis=1, tiled=True)
    summed = jnp.sum(received, axis=1)
    denom = jnp.take(ab_energy, my_source)[None, :] - ij_energy[:, None]
    return jnp.where(my_valid[None, :], summed / denom, 0.0)


def solution(mesh):
    placed = (P("blk", "vslab", None), P("vslab", None, "blk"), P("blk"), P(), P(), P())
    return jax.shard_map(
        on_device, mesh=mesh, in_specs=placed, out_specs=P(None, ("blk", "vslab")), check_vma=False
    )
```

profile of v0, /device:TPU:1, one launch (start us, length us, event | category | flops | bytes accessed | tf_op | source)
XLA Modules:
  0.0 425.9 jit_solution(9916567833174694342)
XLA Ops:
  6.5 0.0 copy-start
  6.5 0.0 all-gather.2.cloned.1.call-start
  6.5 0.7 all-gather.2.cloned.1.call-update
  7.3 0.8 select_reduce_fusion.5
  8.0 0.1 select_reduce_fusion.4
  8.2 0.1 compare_select_fusion.2
  8.2 0.1 reshape.187
  8.3 0.8 select_reduce_fusion.3
  9.1 0.9 select_reduce_fusion.1
  10.0 0.7 fusion.7
  10.6 0.1 select_reduce_fusion
  10.8 2.4 scatter_custom_fusion
  13.2 9.5 %gather_fusion = s32[1536]{0:T(1024)S(1)} fusion(s32[512]{0:T(512)S(1)} %scatter_custom_fusion, s32[2048]{0:T(1024)S(1)} %pad_clamp_fusion.1), kind=kCustom, calls=%fused_computation | custom fusion | bytes 18432 | tf_op jit(solution)/shard_map/gather | solution.py:32
  22.7 0.1 reshape.186
  22.8 0.1 iota_compare_fusion.5
  22.9 251.6 %all-gather.2.cloned.1.call-done = f32[1024,6400]{0,1:T(8,128)} async-done(((f32[128,6400]{0,1:T(8,128)}), f32[1024,6400]{0,1:T(8,128)}) %all-gather.2.cloned.1.call-update) | async-done | bytes 26214416 | tf_op jit(solution)/shard_map/all_gather | solution.py:43
  274.5 45.6 %fusion.8 = f32[1024,512]{0,1:T(8,128)S(1)} fusion(f32[1024,6400]{0,1:T(8,128)} %all-gather.2.cloned.1.call-done, f32[6400,512]{1,0:T(8,128)} %bitcast.27), kind=kOutput, calls=%fused_computation.40 | convolution fusion | flops 40265318400 | bytes 41418752 | tf_op jit(solution)/shard_map/dot_general | solution.py:42
  320.0 5.8 %gather_fusion.1 = f32[1536,1024]{1,0:T(8,128)} fusion(f32[1024,512]{0,1:T(8,128)S(1)} %fusion.8, s32[2048]{0:T(1024)S(1)} %pad_clamp_fusion), kind=kCustom, calls=%fused_computation.1 | custom fusion | bytes 12589056 | tf_op jit(solution)/shard_map/jit(_take)/gather | solution.py:52
  325.9 4.9 %select_select_fusion = f32[1024,16,96]{0,2,1:T(8,128)} fusion(f32[1024,16,96]{0,2,1:T(8,128)} %bitcast.23, pred[16,96]{1,0:T(8,128)(4,1)S(1)} %get-tuple-element.10, pred[16,96]{1,0:T(8,128)(4,1)S(1)} %get-tuple-element.9), kind=kLoop, calls=%fused_computation.4 | loop fusion | flops 3145728 | bytes 12585984 | tf_op jit(solution)/shard_map/jit(_where)/select_n | solution.py:53
  330.8 10.4 %all-to-all-start = ((f32[1024,16,96]{0,2,1:T(8,128)}), f32[1024,16,96]{0,2,1:T(8,128)}, u32[]{:S(2)}, u32[]{:S(2)}) async-start(f32[1024,16,96]{0,2,1:T(8,128)} %select_select_fusion), calls=%async_computation | async-start | bytes 12582912 | tf_op jit(solution)/shard_map/all_to_all | solution.py:54
  341.2 0.0 copy-start.1
  341.3 0.0 copy-done
  341.3 1.3 gather_fusion.2
  342.6 72.2 %all-to-all-done = f32[1024,16,96]{0,2,1:T(8,128)} async-done(((f32[1024,16,96]{0,2,1:T(8,128)}), f32[1024,16,96]{0,2,1:T(8,128)}, u32[]{:S(2)}, u32[]{:S(2)}) %all-to-all-start) | async-done | bytes 6291488 | tf_op jit(solution)/shard_map/all_to_all | solution.py:54
  414.8 3.4 reduce_sum.72
  418.2 0.0 copy-done.1
  418.2 0.9 divide_select_fusion
  (9 shorter events, 0.1 us)
Async XLA Ops:
  6.5 334.7 %copy-start = (f32[512]{0:T(512)S(1)}, f32[512]{0:T(512)}, u32[]{:S(2)}) copy-start(f32[512]{0:T(512)} %param.8) | copy-start | bytes 6148
  6.5 267.9 %all-gather.2.cloned.1.call-start = ((), (), s32[]{:S(2)}) async-start(), calls=%async_computation.1 | async-start | bytes 29491200 | tf_op jit(solution)/shard_map/all_gather | solution.py:43
  330.8 84.0 %all-to-all-start = ((f32[1024,16,96]{0,2,1:T(8,128)}), f32[1024,16,96]{0,2,1:T(8,128)}, u32[]{:S(2)}, u32[]{:S(2)}) async-start(f32[1024,16,96]{0,2,1:T(8,128)} %select_select_fusion), calls=%async_computation | async-start | bytes 12582912 | tf_op jit(solution)/shard_map/all_to_all | solution.py:54
  341.2 76.9 %copy-start.1 = (f32[1024]{0:T(1024)S(1)}, f32[1024]{0:T(1024)}, u32[]{:S(2)}) copy-start(f32[1024]{0:T(1024)} %param.9) | copy-start | bytes 12292
Sparse Core Ops, SparseCore 0:
  8.9 265.4 all-gather.1
where the time goes:
time: 426 us
  waiting for transfers between devices  324 us (76%)
  matrix products  45.6 us (11%)
  local copies, waits for them, and re-layouts  19.2 us (5%)
  between operations  13.5 us (3%)
  other arithmetic  12.7 us (3%)
  starting transfers between devices  10.4 us (2%)
    all_gather x1, waiting for transfers between devices, on_device(): lax.all_gather(t_tile, 'blk', axis=0, tiled=True)  252 us
    all_to_all x1, waiting for transfers between devices, on_device(): lax.all_to_all(packed, 'vslab', split_axis=1, concat_axis=1, tiled=True)  72.2 us
    dot_general x1, matrix products, on_device(): jnp.dot(lax.all_gather(t_tile, 'blk', axis=0, tiled=True), v_matrix, prec...  45.6 us
    all_to_all x1, starting transfers between devices, on_device(): lax.all_to_all(packed, 'vslab', split_axis=1, concat_axis=1, tiled=True)  10.4 us
    gather x2, local copies, waits for them, and re-layouts, slot_tables(): source = perm[index]  9.54 us
  transfers between devices with their start and end apart: 2, of which 2 were waited for; matrix products, arithmetic and copies ran while one was open for 4% of the time, Pallas kernels for 0%

commit v1 on v0

--- a/solution.py
+++ b/solution.py
@@ -40,7 +40,9 @@
     v_matrix = integrals.reshape(-1, rows)
     t_tile = amplitudes.reshape(amplitudes.shape[0], -1)
     ladder = jnp.dot(
-        lax.all_gather(t_tile, "blk", axis=0, tiled=True),
+        jnp.concatenate(
+            lax.all_to_all(jnp.stack([t_tile] * lax.axis_size("blk")), "blk", 0, 0), axis=0
+        ),
         v_matrix,
         precision=lax.Precision.HIGHEST,
         preferred_element_type=jnp.float32,

time: 426 us -> 557 us (1.31)
  the two profiles are of different devices: /device:TPU:1 before, /device:TPU:6 now
where the time goes in v1:
time: 557 us; the launch traced here: 556 us
  waiting for transfers between devices  452 us (81%)
  matrix products  45.8 us (8%)
  local copies, waits for them, and re-layouts  33.7 us (6%)
  starting transfers between devices  15.2 us (3%)
  other arithmetic  10 us (2%)
    all_to_all x1, waiting for transfers between devices, on_device(): lax.all_to_all(jnp.stack([t_tile] * lax.axis_size('blk')), 'blk', 0, 0)  379 us
    all_to_all x1, waiting for transfers between devices, on_device(): lax.all_to_all(packed, 'vslab', split_axis=1, concat_axis=1, tiled=True)  73 us
    dot_general x1, matrix products, on_device(): jnp.dot(jnp.concatenate(lax.all_to_all(jnp.stack([t_tile] * lax.axis_size...  45.8 us
    another operation x2, local copies, waits for them, and re-layouts, on_device(): jnp.stack([t_tile] * lax.axis_size('blk'))  14.3 us
  transfers between devices with their start and end apart: 2, of which 2 were waited for; matrix products, arithmetic and copies ran while one was open for 3% of the time, Pallas kernels for 0%

profile of v1, /device:TPU:6, one launch (start us, length us, event | category | flops | bytes accessed | tf_op | source)
XLA Modules:
  0.0 556.5 jit_solution(18389241839099485380)
XLA Ops:
  0.0 0.0 copy-start
  0.0 3.4 copy.11
  3.4 10.9 %stack.3 = f32[8,128,6400]{2,1,0:T(8,128)} broadcast(f32[128,6400]{1,0:T(8,128)S(1)} %copy.11), dimensions={1,2} | broadcast | bytes 29491200 | tf_op jit(solution)/shard_map/stack | solution.py:44
  14.3 0.0 copy-start.2
  14.3 0.0 copy-start.3
  14.3 6.9 %all-to-all-start = ((f32[8,128,6400]{2,1,0:T(8,128)}), f32[8,128,6400]{2,1,0:T(8,128)}, u32[]{:S(2)}, u32[]{:S(2)}) async-start(f32[8,128,6400]{2,1,0:T(8,128)} %stack.3), calls=%async_computation | async-start | bytes 52428800 | tf_op jit(solution)/shard_map/all_to_all | solution.py:44
  21.2 0.0 copy-done.2
  21.2 0.0 copy-done.3
  21.2 0.1 select_reduce_fusion.5
  21.3 0.1 select_reduce_fusion.4
  21.5 0.1 compare_select_fusion.2
  21.5 0.1 reshape.189
  21.6 0.1 select_reduce_fusion.3
  21.7 0.2 select_reduce_fusion.1
  21.9 0.1 select_reduce_fusion
  22.0 2.6 scatter_custom_fusion
  24.7 9.5 %gather_fusion = s32[1536]{0:T(1024)S(1)} fusion(s32[512]{0:T(512)S(1)} %scatter_custom_fusion, s32[2048]{0:T(1024)S(1)} %pad_clamp_fusion.1), kind=kCustom, calls=%fused_computation | custom fusion | bytes 18432 | tf_op jit(solution)/shard_map/gather | solution.py:32
  34.1 0.1 reshape.188
  34.2 0.1 iota_compare_fusion.5
  34.3 378.6 %all-to-all-done = f32[8,128,6400]{2,1,0:T(8,128)} async-done(((f32[8,128,6400]{2,1,0:T(8,128)}), f32[8,128,6400]{2,1,0:T(8,128)}, u32[]{:S(2)}, u32[]{:S(2)}) %all-to-all-start) | async-done | bytes 26214432 | tf_op jit(solution)/shard_map/all_to_all | solution.py:44
  412.9 45.8 %fusion.8 = f32[1024,512]{0,1:T(8,128)S(1)} fusion(f32[1024,6400]{1,0:T(8,128)} %bitcast.4, f32[6400,512]{1,0:T(8,128)} %bitcast.28), kind=kOutput, calls=%fused_computation.40 | convolution fusion | flops 40265318400 | bytes 41418752 | tf_op jit(solution)/shard_map/dot_general | solution.py:42
  458.7 5.8 %gather_fusion.1 = f32[1536,1024]{1,0:T(8,128)} fusion(f32[1024,512]{0,1:T(8,128)S(1)} %fusion.8, s32[2048]{0:T(1024)S(1)} %pad_clamp_fusion), kind=kCustom, calls=%fused_computation.1 | custom fusion | bytes 12589056 | tf_op jit(solution)/shard_map/jit(_take)/gather | solution.py:54
  464.6 4.9 select_select_fusion
  469.5 8.3 %all-to-all-start.1 = ((f32[1024,16,96]{0,2,1:T(8,128)}), f32[1024,16,96]{0,2,1:T(8,128)}, u32[]{:S(2)}, u32[]{:S(2)}) async-start(f32[1024,16,96]{0,2,1:T(8,128)} %select_select_fusion), calls=%async_computation.1 | async-start | bytes 12582912 | tf_op jit(solution)/shard_map/all_to_all | solution.py:56
  477.9 0.0 copy-start.1
  477.9 0.0 copy-done
  477.9 1.3 gather_fusion.2
  479.2 73.0 %all-to-all-done.1 = f32[1024,16,96]{0,2,1:T(8,128)} async-done(((f32[1024,16,96]{0,2,1:T(8,128)}), f32[1024,16,96]{0,2,1:T(8,128)}, u32[]{:S(2)}, u32[]{:S(2)}) %all-to-all-start.1) | async-done | bytes 6291488 | tf_op jit(solution)/shard_map/all_to_all | solution.py:56
  552.2 3.4 reduce_sum.72
  555.6 0.0 copy-done.1
  555.6 0.9 divide_select_fusion
  (10 shorter events, 0.1 us)
Async XLA Ops:
  0.0 477.9 %copy-start = (f32[512]{0:T(512)S(1)}, f32[512]{0:T(512)}, u32[]{:S(2)}) copy-start(f32[512]{0:T(512)} %param.8) | copy-start | bytes 6148
  14.3 6.9 %copy-start.2 = (s32[32]{0:T(128)S(1)}, s32[32]{0:T(128)}, u32[]{:S(2)}) copy-start(s32[32]{0:T(128)} %param.11) | copy-start | bytes 388
  14.3 6.9 %copy-start.3 = (s32[32]{0:T(128)S(1)}, s32[32]{0:T(128)}, u32[]{:S(2)}) copy-start(s32[32]{0:T(128)} %param.10) | copy-start | bytes 388
  14.3 398.6 %all-to-all-start = ((f32[8,128,6400]{2,1,0:T(8,128)}), f32[8,128,6400]{2,1,0:T(8,128)}, u32[]{:S(2)}, u32[]{:S(2)}) async-start(f32[8,128,6400]{2,1,0:T(8,128)} %stack.3), calls=%async_computation | async-start | bytes 52428800 | tf_op jit(solution)/shard_map/all_to_all | solution.py:44
  469.5 82.7 %all-to-all-start.1 = ((f32[1024,16,96]{0,2,1:T(8,128)}), f32[1024,16,96]{0,2,1:T(8,128)}, u32[]{:S(2)}, u32[]{:S(2)}) async-start(f32[1024,16,96]{0,2,1:T(8,128)} %select_select_fusion), calls=%async_computation.1 | async-start | bytes 12582912 | tf_op jit(solution)/shard_map/all_to_all | solution.py:56
  477.9 77.7 %copy-start.1 = (f32[1024]{0:T(1024)S(1)}, f32[1024]{0:T(1024)}, u32[]{:S(2)}) copy-start(f32[1024]{0:T(1024)} %param.9) | copy-start | bytes 12292
